TPU v7x, 32 devices: a whole 2x2x4 slice. The times are simulated.
32 devices in a mesh: groups: 2 (over y), ctx: 4 (over x, core), head: 4 (over z).
Axes of the slice: x: 2, y: 2, z: 4, core: 2. Of those that a mesh axis runs over, the one named last changes fastest.
Arguments:
- span_query: bfloat16 [4, 128, 64, 128], P('groups', 'ctx', 'head'), parts along dimension 0, may hold values from -5 to 5
- span_key: bfloat16 [4, 128, 8, 128], P('groups', 'ctx', 'head'), parts along dimension 0, may hold values from -15 to 15
- span_value: bfloat16 [4, 128, 8, 128], P('groups', 'ctx', 'head'), parts along dimension 0, may hold values from -6 to 6
- prefix_key: bfloat16 [64, 128, 8, 128], P(('groups', 'ctx'), None, 'head'), parts along dimension 0, may hold values from -15 to 15
- prefix_value: bfloat16 [64, 128, 8, 128], P(('groups', 'ctx'), None, 'head'), parts along dimension 0, may hold values from -6 to 6
- page_table: int32 [4, 16], P('groups', 'ctx'), parts along dimension 0, may hold values from 0 to 7, as said below
- decode_query: bfloat16 [8, 32, 64, 128], P('groups', 'ctx', 'head'), parts along dimension 0, may hold values from -5 to 5
- decode_key: bfloat16 [8, 32, 8, 128], P('groups', 'ctx', 'head'), parts along dimension 0, may hold values from -15 to 15
- decode_value: bfloat16 [8, 32, 8, 128], P('groups', 'ctx', 'head'), parts along dimension 0, may hold values from -6 to 6
- sample_prompt: int32 [64], P('groups'), parts along dimension 0, may hold values from 0 to 1, as said below
- out_weight: bfloat16 [8192, 8192], P('head', 'ctx'), may hold values from -0.25 to 0.25
Outputs:
- span_out: bfloat16 [4, 128, 8192], P('groups', None, 'ctx'), parts along dimension 0
- decode_out: bfloat16 [8, 32, 8192], P('groups', None, 'ctx'), parts along dimension 0
There are 2 independent parts, one for each index of `groups`. A program takes and returns all parts, laid end to end along the dimension named above; an argument that names none is the same for every part. Nothing has to cross between parts.
Inputs may be any that keep to these rules, and one draw needn't show every extreme that they name: `page_table`: within each block of 4 columns (one index of ctx) the entries of both prompts together are a permutation of 0 to 7. `sample_prompt`: every prompt has exactly 16 samples.
All inputs are finite; a program needn't handle non-finite values.
Results may differ from a plain program's by a relative error of at most 0.0075.
Values may be sent and summed in bfloat16 or wider, within the bound.
A program may use at most 64 MiB of HBM per device.

v0:
```python
import math

import jax
import jax.numpy as jnp
from jax import lax
from jax.sharding import PartitionSpec as P

negative_floor = -1e30


def absorb(softmax_state, queries, key_rows, value_rows, allowed):
    running_max, running_sum, weighted = softmax_state
    scores = jnp.einsum("brd,bnd->brn", queries, key_rows, preferred_element_type=jnp.float32) * (
        1.0 / math.sqrt(queries.shape[-1])
    )
    if allowed is not None:
        scores = jnp.where(allowed, scores, negative_floor)
    new_max = jnp.maximum(running_max, jnp.max(scores, axis=-1))
    factor = jnp.exp(running_max - new_max)
    weights = jnp.exp(scores - new_max[..., None])
    running_sum = running_sum * factor + jnp.sum(weights, axis=-1)
    weighted = weighted * factor[..., None] + jnp.einsum(
        "brn,bnd->brd", weights.astype(jnp.bfloat16), value_rows, preferred_element_type=jnp.float32
    )
    return (new_max, running_sum, weighted)


def sweep(softmax_state, queries, key_rows, value_rows, block_width):
    total_keys = key_rows.shape[1]
    block_width = math.gcd(total_keys, block_width)

    def one_block(state_in, block_start):
        key_block = lax.dynamic_slice_in_dim(key_rows, block_start, block_width, 1)
        value_block = lax.dynamic_slice_in_dim(value_rows, block_start, block_width, 1)
        return (absorb(state_in, queries, key_block, value_block, None), None)

    starts = jnp.arange(total_keys // block_width, dtype=jnp.int32) * block_width
    softmax_state, unused = lax.scan(one_block, softmax_state, starts)
    return softmax_state


def empty_state(head_batch, row_count, head_depth):
    return (
        jnp.full((head_batch, row_count), negative_floor, jnp.float32),
        jnp.zeros((head_batch, row_count), jnp.float32),
        jnp.zeros((head_batch, row_count, head_depth), jnp.float32),
    )


def own_steps(softmax_state, queries_five, own_key, own_value):
    running_max, running_sum, weighted = softmax_state
    key_rows = own_key.transpose(2, 1, 0, 3)
    value_rows = own_value.transpose(2, 1, 0, 3)
    scores = jnp.einsum(
        "ktsgd,ksud->ktsgu", queries_five, key_rows, preferred_element_type=jnp.float32
    ) * (1.0 / math.sqrt(queries_five.shape[-1]))
    step_total = queries_five.shape[1]
    step_ids = jnp.arange(step_total, dtype=jnp.int32)
    allowed = (step_ids[None, :] <= step_ids[:, None])[None, :, None, None, :]
    scores = jnp.where(allowed, scores, negative_floor)
    new_max = jnp.maximum(running_max, jnp.max(scores, axis=-1))
    factor = jnp.exp(running_max - new_max)
    weights = jnp.exp(scores - new_max[..., None])
    running_sum = running_sum * factor + jnp.sum(weights, axis=-1)
    weighted = weighted * factor[..., None] + jnp.einsum(
        "ktsgu,ksud->ktsgd",
        weights.astype(jnp.bfloat16),
        value_rows,
        preferred_element_type=jnp.float32,
    )
    return (weighted / running_sum[..., None]).astype(jnp.bfloat16)


def shards(
    span_query,
    span_key,
    span_value,
    prefix_key,
    prefix_value,
    page_table,
    decode_query,
    decode_key,
    decode_value,
    sample_prompt,
    out_weight,
):
    prompts, span_dev, heads_dev, head_depth = span_query.shape
    kv_heads = span_key.shape[2]
    group_size = heads_dev // kv_heads
    steps_count = decode_query.shape[0]
    samples_dev = decode_query.shape[1]
    head_batch = prompts * kv_heads
    ctx_index = lax.axis_index("ctx")
    slot_rows = page_table.reshape(-1)
    local_keys = (
        jnp.take(prefix_key, slot_rows, axis=0)
        .reshape(prompts, -1, kv_heads, head_depth)
        .transpose(0, 2, 1, 3)
    )
    local_values = (
        jnp.take(prefix_value, slot_rows, axis=0)
        .reshape(prompts, -1, kv_heads, head_depth)
        .transpose(0, 2, 1, 3)
    )
    span_rows = (
        span_query.reshape(prompts, span_dev, kv_heads, group_size, head_depth)
        .transpose(0, 2, 1, 3, 4)
        .reshape(head_batch, span_dev * group_size, head_depth)
    )
    span_keys_all, span_values_all = (
        lax.all_gather(span_key, "ctx", axis=1, tiled=True),
        lax.all_gather(span_value, "ctx", axis=1, tiled=True),
    )
    span_total = span_keys_all.shape[1]
    span_key_rows = span_keys_all.transpose(0, 2, 1, 3).reshape(head_batch, span_total, head_depth)
    span_value_rows = span_values_all.transpose(0, 2, 1, 3).reshape(
        head_batch, span_total, head_depth
    )
    query_pos = (
        ctx_index * span_dev + jnp.arange(span_dev * group_size, dtype=jnp.int32) // group_size
    )
    causal = (jnp.arange(span_total, dtype=jnp.int32)[None, :] <= query_pos[:, None])[None]
    decode_five = decode_query.reshape(
        steps_count, samples_dev, kv_heads, group_size, head_depth
    ).transpose(2, 0, 1, 3, 4)
    prefill_state = empty_state(head_batch, span_dev * group_size, head_depth)
    prompt_keys_all, prompt_values_all = (
        lax.all_gather(local_keys, "ctx", axis=2, tiled=True),
        lax.all_gather(local_values, "ctx", axis=2, tiled=True),
    )
    prefix_len = prompt_keys_all.shape[2]
    key_rows = prompt_keys_all.reshape(head_batch, prefix_len, head_depth)
    value_rows = prompt_values_all.reshape(head_batch, prefix_len, head_depth)
    prefill_state = sweep(prefill_state, span_rows, key_rows, value_rows, 2048)
    decode_flat = decode_five.reshape(kv_heads, -1, head_depth)
    decode_batch = jnp.broadcast_to(decode_flat[None], (prompts,) + decode_flat.shape).reshape(
        head_batch, -1, head_depth
    )
    decode_state = empty_state(head_batch, decode_flat.shape[1], head_depth)
    decode_state = sweep(decode_state, decode_batch, key_rows, value_rows, 2048)
    decode_state = sweep(decode_state, decode_batch, span_key_rows, span_value_rows, span_total)
    own_prompts = lax.dynamic_slice_in_dim(sample_prompt, ctx_index * samples_dev, samples_dev)
    chosen = (
        own_prompts[None, None, None, :, None]
        == jnp.arange(prompts, dtype=jnp.int32)[:, None, None, None, None]
    )

    def select_prompt(member):
        shaped = member.reshape(
            (prompts, kv_heads, steps_count, samples_dev, group_size) + member.shape[2:]
        )
        select_mask = chosen.reshape(chosen.shape + (1,) * (shaped.ndim - 5))
        return jnp.sum(jnp.where(select_mask, shaped, 0.0), axis=0)

    decode_state = tuple((select_prompt(member) for member in decode_state))
    prefill_state = absorb(prefill_state, span_rows, span_key_rows, span_value_rows, causal)
    span_mixed = (prefill_state[2] / prefill_state[1][..., None]).astype(jnp.bfloat16)
    span_attn = (
        span_mixed.reshape(prompts, kv_heads, span_dev, group_size, head_depth)
        .transpose(0, 2, 1, 3, 4)
        .reshape(prompts * span_dev, heads_dev * head_depth)
    )
    decode_mixed = own_steps(decode_state, decode_five, decode_key, decode_value)
    decode_attn = decode_mixed.transpose(1, 2, 0, 3, 4).reshape(
        steps_count * samples_dev, heads_dev * head_depth
    )
    rows_local = jnp.concatenate([span_attn, decode_attn], axis=0)
    projected = jnp.dot(
        lax.all_gather(rows_local, "ctx", axis=0, tiled=True),
        out_weight,
        preferred_element_type=jnp.float32,
    )
    share = lax.psum_scatter(projected, "head", scatter_dimension=0, tiled=True).astype(
        jnp.bfloat16
    )
    summed = lax.all_gather(share, "head", axis=0, tiled=True)
    rows_dev = rows_local.shape[0]
    blocks_by_ctx = summed.reshape(-1, rows_dev, summed.shape[-1])
    ctx_count = blocks_by_ctx.shape[0]
    span_out = (
        blocks_by_ctx[:, : prompts * span_dev]
        .reshape(ctx_count, prompts, span_dev, -1)
        .transpose(1, 0, 2, 3)
        .reshape(prompts, ctx_count * span_dev, -1)
    )
    decode_out = (
        blocks_by_ctx[:, prompts * span_dev :]
        .reshape(ctx_count, steps_count, samples_dev, -1)
        .transpose(1, 0, 2, 3)
        .reshape(steps_count, ctx_count * samples_dev, -1)
    )
    return (span_out, decode_out)


def solution(mesh):
    return jax.shard_map(
        shards,
        mesh=mesh,
        in_specs=(
            P("groups", "ctx", "head", None),
            P("groups", "ctx", "head", None),
            P("groups", "ctx", "head", None),
            P(("groups", "ctx"), None, "head", None),
            P(("groups", "ctx"), None, "head", None),
            P("groups", "ctx"),
            P("groups", "ctx", "head", None),
            P("groups", "ctx", "head", None),
            P("groups", "ctx", "head", None),
            P("groups"),
            P("head", "ctx"),
        ),
        out_specs=(P("groups", None, "ctx"), P("groups", None, "ctx")),
        check_vma=False,
    )
```

profile of v0, /device:TPU:0, one launch (start us, length us, event | category | flops | bytes accessed | tf_op | source)
XLA Modules:
  0.0 230.2 jit_solution(950019936043663763)
XLA Ops:
  7.3 0.8 reshape.229
  8.1 0.2 copy-done
  8.3 1.6 gather_fusion
  9.9 2.6 %gather_fusion.1 = bf16[8,128,2,128]{3,2,1,0:T(2,128)(2,1)S(1)} fusion(bf16[8,128,2,128]{3,2,1,0:T(2,128)(2,1)} %param.17, s32[1024]{0:T(1024)S(1)} %pad_clamp_fusion), kind=kCustom, calls=%fused_computation.1.clone | custom fusion | bytes 1048608 | tf_op jit(solution)/shard_map/jit(_take)/gather | solution.py:101
  12.6 1.0 broadcast_select_fusion.1
  13.6 0.9 copy.135
  14.5 0.9 copy.134
  15.5 6.7 %all_gather.20 = bf16[2,128,2,128]{3,2,1,0:T(2,128)(2,1)S(1)} all-gather(bf16[2,32,2,128]{3,2,1,0:T(2,128)(2,1)} %param.14), channel_id=1, replica_groups=mesh['groups'=2,'ctx'=4,'head'=4] {'ctx'}, dimensions={1}, use_global_device_ids=true | all-gather | bytes 163840 | tf_op jit(solution)/shard_map/all_gather | solution.py:111
  22.2 0.9 copy.89
  23.2 0.2 fusion.56
  23.4 6.2 %all_gather.21 = bf16[2,128,2,128]{3,2,1,0:T(2,128)(2,1)S(1)} all-gather(bf16[2,32,2,128]{3,2,1,0:T(2,128)(2,1)S(1)} %copy-done.9), channel_id=1, replica_groups=mesh['groups'=2,'ctx'=4,'head'=4] {'ctx'}, dimensions={1}, use_global_device_ids=true | all-gather | bytes 163840 | tf_op jit(solution)/shard_map/all_gather | solution.py:112
  29.8 0.7 reduce_max.56
  30.6 0.5 iota_compare_fusion.2
  31.1 2.0 fusion.57
  33.0 0.2 fusion.58
  33.3 7.3 %all-gather.5.cloned.1.call-done = bf16[2,2,2048,128]{3,2,1,0:T(8,128)(2,1)} async-done(((bf16[2,2,512,128]{3,2,1,0:T(8,128)(2,1)}), bf16[2,2,2048,128]{3,2,1,0:T(8,128)(2,1)}) %all-gather.5.cloned.1.call-update) | async-done | bytes 2097168 | tf_op jit(solution)/shard_map/all_gather | solution.py:128
  40.6 2.9 %bitcast_reduce_fusion.1 = (f32[4,256]{1,0:T(4,128)S(1)}, f32[4,2048,256]{2,1,0:T(8,128)S(1)}) fusion(bf16[4,2048,128]{2,1,0:T(8,128)(2,1)} %bitcast.123, bf16[4,256,128]{2,1,0:T(8,128)(2,1)S(1)} %bitcast.131), kind=kOutput, calls=%fused_computation.6 | convolution fusion | flops 541064192 | bytes 10752000 | tf_op jit(solution)/shard_map/while/body/eval_jaxpr/brd,bnd->brn/dot_general | solution.py:13
  43.6 3.4 %copy-done.1 = f32[4,2048,256]{2,1,0:T(8,128)} copy-done((f32[4,2048,256]{2,1,0:T(8,128)}, f32[4,2048,256]{2,1,0:T(8,128)S(1)}, u32[]{:S(2)}) %copy-start.1) | copy-done | bytes 8388632
  47.0 1.4 fusion.2
  48.4 0.6 multiply_add_fusion
  49.0 5.1 %bitcast_reduce_fusion = (f32[4,256]{1,0:T(4,128)}, f32[4,2048,256]{2,1,0:T(8,128)}) fusion(bf16[4,2048,128]{2,1,0:T(8,128)(2,1)S(1)} %bitcast.124, bf16[4,256,128]{2,1,0:T(8,128)(2,1)S(1)} %bitcast.129), kind=kOutput, calls=%fused_computation.3 | convolution fusion | flops 541064192 | bytes 10752000 | tf_op jit(solution)/shard_map/while/body/eval_jaxpr/brd,bnd->brn/dot_general | solution.py:13
  54.1 11.3 %all-gather.7.cloned.1.call-done = bf16[2,2,2048,128]{3,2,1,0:T(8,128)(2,1)} async-done(((bf16[2,2,512,128]{3,2,1,0:T(8,128)(2,1)}), bf16[2,2,2048,128]{3,2,1,0:T(8,128)(2,1)}) %all-gather.7.cloned.1.call-update) | async-done | bytes 2097168 | tf_op jit(solution)/shard_map/all_gather | solution.py:129
  65.4 5.2 %fusion.25 = f32[4,256,128]{2,1,0:T(8,128)S(1)} fusion(bf16[4,2048,128]{2,1,0:T(8,128)(2,1)} %bitcast.125, f32[4,2048,256]{2,1,0:T(8,128)} %copy-done.1, f32[4,256]{1,0:T(4,128)S(1)} %get-tuple-element.62, f32[4,256]{1,0:T(4,128)S(1)} %get-tuple-element.48, f32[4,256]{1,0:T(4,128)S(1)} %get-tuple-element.60), kind=kOutput, calls=%fused_computation.27 | convolution fusion | flops 543424512 | bytes 11022336 | tf_op jit(solution)/shard_map/while/body/eval_jaxpr/brn,bnd->brd/dot_general | solution.py:22
  70.6 0.3 fusion.28
  71.0 0.7 copy.136
  71.7 1.1 reshape.239
  72.8 1.3 fusion.54
  74.1 0.7 max.91
  74.8 4.8 %fusion.4 = f32[4,256]{1,0:T(4,128)S(1)} fusion(f32[4,2048,256]{2,1,0:T(8,128)} %get-tuple-element.84, f32[4,256]{1,0:T(4,128)S(1)} %get-tuple-element.71), kind=kLoop, calls=%fused_computation.10 | loop fusion | flops 6290432 | bytes 8396800 | tf_op jit(solution)/shard_map/while/body/eval_jaxpr/reduce_sum | solution.py:21
  79.5 0.7 reduce_sum.94
  80.3 0.7 reduce_sum.96
  81.1 1.1 select_reduce_fusion.1
  82.1 0.8 copy_maximum_fusion
  82.9 1.0 fusion.43
  83.9 0.8 bitcast_add_fusion
  84.8 4.6 %fusion.22 = f32[4,256,128]{2,1,0:T(8,128)S(1)} fusion(bf16[4,2048,128]{2,1,0:T(8,128)(2,1)S(1)} %bitcast.126, f32[4,2048,256]{2,1,0:T(8,128)} %get-tuple-element.84, f32[4,256]{1,0:T(4,128)S(1)} %get-tuple-element.71, f32[4,256]{1,0:T(4,128)S(1)} %get-tuple-element.59, f32[4,256]{1,0:T(4,128)} %get-tuple-element.70), kind=kOutput, calls=%fused_computation.26 | convolution fusion | flops 543424512 | bytes 11022336 | tf_op jit(solution)/shard_map/while/body/eval_jaxpr/brn,bnd->brd/dot_general | solution.py:22
  89.3 0.3 convolution_add_fusion
  89.8 0.3 fusion.31
  90.2 0.8 pad_maximum_fusion
  91.0 0.3 reduce-scatter.2.cloned.1.call-start
  91.3 19.5 %all-gather.9.cloned.1.call-done = bf16[384,2048]{1,0:T(8,128)(2,1)} async-done(((bf16[96,2048]{1,0:T(8,128)(2,1)}), bf16[384,2048]{1,0:T(8,128)(2,1)}) %all-gather.9.cloned.1.call-update) | async-done | bytes 1572880 | tf_op jit(solution)/shard_map/all_gather | solution.py:169
  110.8 8.9 %fusion.59 = f32[384,2048]{1,0:T(8,128)} fusion(bf16[384,2048]{1,0:T(8,128)(2,1)} %all-gather.9.cloned.1.call-done, bf16[2048,2048]{1,0:T(8,128)(2,1)} %param.23), kind=kOutput, calls=%fused_computation.93 | convolution fusion | flops 3221225472 | bytes 13107200 | tf_op jit(solution)/shard_map/dot_general | solution.py:168
  119.8 60.4 %reduce-scatter.2.cloned.1.call-done = f32[96,2048]{1,0:T(8,128)} async-done(((f32[384,2048]{1,0:T(8,128)}), f32[96,2048]{1,0:T(8,128)}) %reduce-scatter.2.cloned.1.call-update) | async-done | bytes 786448 | tf_op jit(solution)/shard_map/reduce_scatter | solution.py:173
  180.2 1.9 convert_element_type.35
  182.1 37.3 %all-gather.11.cloned.1.call-done = bf16[384,2048]{1,0:T(8,128)(2,1)} async-done(((bf16[96,2048]{1,0:T(8,128)(2,1)}), bf16[384,2048]{1,0:T(8,128)(2,1)}) %all-gather.11.cloned.1.call-update) | async-done | bytes 1572880 | tf_op jit(solution)/shard_map/all_gather | solution.py:176
  219.4 1.3 slice.12
  220.7 1.9 copy_bitcast_fusion
  222.6 1.0 copy.103
  (57 shorter events, 1.0 us)
Async XLA Ops:
  7.2 1.2 copy-start
  7.2 23.9 %copy-start.8 = (bf16[4,8,16,128]{3,2,1,0:T(8,128)(2,1)S(1)}, bf16[4,8,16,128]{3,2,1,0:T(8,128)(2,1)}, u32[]{:S(2)}) copy-start(bf16[4,8,16,128]{3,2,1,0:T(8,128)(2,1)} %param.19) | copy-start | bytes 393220
  7.2 16.2 %copy-start.9 = (bf16[2,32,2,128]{3,2,1,0:T(2,128)(2,1)S(1)}, bf16[2,32,2,128]{3,2,1,0:T(2,128)(2,1)}, u32[]{:S(2)}) copy-start(bf16[2,32,2,128]{3,2,1,0:T(2,128)(2,1)} %param.15) | copy-start | bytes 98308
  7.2 22.5 %copy-start.6 = (bf16[2,32,16,128]{3,2,1,0:T(8,128)(2,1)S(1)}, bf16[2,32,16,128]{3,2,1,0:T(8,128)(2,1)}, u32[]{:S(2)}) copy-start(bf16[2,32,16,128]{3,2,1,0:T(8,128)(2,1)} %param.13) | copy-start | bytes 786436
  7.2 23.3 %copy-start.14 = (s32[32]{0:T(128)S(1)}, s32[32]{0:T(128)}, u32[]{:S(2)}) copy-start(s32[32]{0:T(128)} %param.22) | copy-start | bytes 388
  7.2 23.9 %copy-start.12 = (bf16[4,8,2,128]{3,2,1,0:T(2,128)(2,1)S(1)}, bf16[4,8,2,128]{3,2,1,0:T(2,128)(2,1)}, u32[]{:S(2)}) copy-start(bf16[4,8,2,128]{3,2,1,0:T(2,128)(2,1)} %param.20) | copy-start | bytes 49156
  7.2 33.4 %all-gather.5.cloned.1.call-start = ((), (), s32[]{:S(2)}) async-start(), calls=%async_computation.1 | async-start | bytes 2621440 | tf_op jit(solution)/shard_map/all_gather | solution.py:128
  14.5 50.9 %all-gather.7.cloned.1.call-start = ((), (), s32[]{:S(2)}) async-start(), calls=%async_computation.2 | async-start | bytes 2621440 | tf_op jit(solution)/shard_map/all_gather | solution.py:129
  15.4 95.4 %all-gather.9.cloned.1.call-start = ((), (), s32[]{:S(2)}) async-start(), calls=%async_computation.3 | async-start | bytes 1966080 | tf_op jit(solution)/shard_map/all_gather | solution.py:169
  33.3 15.1 %copy-start.4 = (f32[4,256,128]{1,2,0:T(8,128)}, f32[4,256,128]{1,2,0:T(8,128)S(1)}, u32[]{:S(2)}) copy-start(f32[4,256,128]{1,2,0:T(8,128)S(1)} %get-tuple-element.90) | copy-start | bytes 1572868
  43.5 3.5 %copy-start.1 = (f32[4,2048,256]{2,1,0:T(8,128)}, f32[4,2048,256]{2,1,0:T(8,128)S(1)}, u32[]{:S(2)}) copy-start(f32[4,2048,256]{2,1,0:T(8,128)S(1)} %get-tuple-element.88) | copy-start | bytes 25165828
  43.5 5.5 %copy-start.2 = (bf16[2,2,2048,128]{3,2,1,0:T(8,128)(2,1)S(1)}, bf16[2,2,2048,128]{3,2,1,0:T(8,128)(2,1)}, u32[]{:S(2)}) copy-start(bf16[2,2,2048,128]{3,2,1,0:T(8,128)(2,1)} %all-gather.5.cloned.1.call-done) | copy-start | bytes 6291460
  54.1 16.6 %copy-start.10 = (f32[4,256]{1,0:T(4,128)S(1)}, f32[4,256]{1,0:T(4,128)}, u32[]{:S(2)}) copy-start(f32[4,256]{1,0:T(4,128)} %get-tuple-element.47) | copy-start | bytes 12292
  65.4 5.3 %copy-start.5 = (f32[4,256,128]{1,2,0:T(8,128)S(1)}, f32[4,256,128]{1,2,0:T(8,128)}, u32[]{:S(2)}) copy-start(f32[4,256,128]{1,2,0:T(8,128)} %copy-done.4) | copy-start | bytes 1572868
  70.6 14.2 %copy-start.3 = (bf16[2,2,2048,128]{3,2,1,0:T(8,128)(2,1)S(1)}, bf16[2,2,2048,128]{3,2,1,0:T(8,128)(2,1)}, u32[]{:S(2)}) copy-start(bf16[2,2,2048,128]{3,2,1,0:T(8,128)(2,1)} %all-gather.7.cloned.1.call-done) | copy-start | bytes 6291460
  81.1 8.6 %copy-start.11 = (pred[2,8]{1,0:T(4,128)(4,1)S(1)}, pred[2,8]{1,0:T(4,128)(4,1)}, u32[]{:S(2)}) copy-start(pred[2,8]{1,0:T(4,128)(4,1)} %iota_compare_fusion.2) | copy-start | bytes 52
  81.1 8.7 %copy-start.7 = (f32[2,4,8,8,4]{3,4,1,2,0:T(4,128)S(1)}, f32[2,4,8,8,4]{3,4,1,2,0:T(4,128)}, u32[]{:S(2)}) copy-start(f32[2,4,8,8,4]{3,4,1,2,0:T(4,128)} %get-tuple-element.86) | copy-start | bytes 24580
  81.1 8.7 %copy-start.13 = (bf16[4,8,2,128]{3,2,1,0:T(2,128)(2,1)S(1)}, bf16[4,8,2,128]{3,2,1,0:T(2,128)(2,1)}, u32[]{:S(2)}) copy-start(bf16[4,8,2,128]{3,2,1,0:T(2,128)(2,1)} %param.21) | copy-start | bytes 49156
  91.0 89.2 %reduce-scatter.2.cloned.1.call-start = ((), (), s32[]{:S(2)}) async-start(), calls=%async_computation.4 | async-start | bytes 3932160 | tf_op jit(solution)/shard_map/reduce_scatter | solution.py:173
  119.8 99.6 %all-gather.11.cloned.1.call-start = ((), (), s32[]{:S(2)}) async-start(), calls=%async_computation.5 | async-start | bytes 1966080 | tf_op jit(solution)/shard_map/all_gather | solution.py:176
Sparse Core Ops, SparseCore 0:
  14.6 25.9 all-gather.4
  42.7 22.5 all-gather.6
  91.1 19.6 all-gather.8
  119.9 60.2 reduce-scatter.1
  182.2 37.1 all-gather.10
where the time goes:
time: 231 us; the launch traced here: 230 us
  waiting for transfers between devices  136 us (59%)
  matrix products  30 us (13%)
  local copies, waits for them, and re-layouts  20.6 us (9%)
  other arithmetic  16.2 us (7%)
  between operations  14.1 us (6%)
  blocking collectives  12.9 us (6%)
    reduce_scatter x1, waiting for transfers between devices, shards(): lax.psum_scatter(projected, 'head', scatter_dimension=0, tiled=True)  60.4 us
    all_gather x1, waiting for transfers between devices, shards(): summed = lax.all_gather(share, 'head', axis=0, tiled=True)  37.3 us
    all_gather x1, waiting for transfers between devices, shards(): lax.all_gather(rows_local, 'ctx', axis=0, tiled=True)  19.5 us
    all_gather x1, waiting for transfers between devices, shards(): lax.all_gather(local_values, 'ctx', axis=2, tiled=True)  11.3 us
    dot_general x4, matrix products, absorb(): jnp.einsum('brn,bnd->brd', weights.astype(jnp.bfloat16), value_rows, pref...  10.4 us
    dot_general x1, matrix products, shards(): jnp.dot(lax.all_gather(rows_local, 'ctx', axis=0, tiled=True), out_weight...  8.94 us
    dot_general x4, matrix products, absorb(): jnp.einsum('brd,bnd->brn', queries, key_rows, preferred_element_type=jnp....  8.4 us
    all_gather x1, waiting for transfers between devices, shards(): lax.all_gather(local_keys, 'ctx', axis=2, tiled=True)  7.31 us
  transfers between devices with their start and end apart: 5, of which 5 were waited for; matrix products, arithmetic and copies ran while one was open for 7% of the time, Pallas kernels for 0%

commit v1 on v0

v1 whole, which is shorter than its diff:
```python
import functools
import math

import jax
import jax.numpy as jnp
from jax import lax
from jax.experimental import pallas as pl
from jax.experimental.pallas import tpu as pltpu
from jax.sharding import PartitionSpec as P

MESH = pl.DeviceIdType.MESH
F32 = jnp.float32
BF16 = jnp.bfloat16
masked_bias = -1e30


def remote(src, dst, send, recv, device):
    return pltpu.make_async_remote_copy(
        src_ref=src,
        dst_ref=dst,
        send_sem=send,
        recv_sem=recv,
        device_id=device,
        device_id_type=MESH,
    )


def kernel(
    dims,
    table,
    keys_in,
    values_in,
    queries_in,
    small_in,
    bias_in,
    pick_in,
    place_in,
    weight_in,
    out_ref,
    kv_send,
    q_send,
    kv_held,
    q_held,
    attended,
    rows_all,
    decode_rows,
    weight,
    part,
    right_out,
    left_out,
    right_in,
    left_in,
    shared,
    kv_ssem,
    kv_rsem,
    q_ssem,
    q_rsem,
    own_sem,
    sib_ssem,
    far_ssem,
    fwd_ssem,
    att_rsem,
    weight_sem,
    right_ssem,
    right_rsem,
    left_ssem,
    left_rsem,
    agr_ssem,
    agl_ssem,
    ag_rsem,
):
    ctx, heads, prompts, kvh, pages, page, span_dev, dec_dev, qh, pair, picked, groups = dims
    me = lax.axis_index("ctx")
    z = lax.axis_index("head")
    share = ctx // prompts
    hd = 128
    chips = ctx // 2
    prefix = pages * page
    blocks = qh // pair
    span = ctx * span_dev
    gcols = weight.shape[2]
    srows = shared.shape[2]

    for g in range(groups):
        pltpu.make_async_copy(
            weight_in.at[:, g * gcols : (g + 1) * gcols], weight.at[g], weight_sem.at[g]
        ).start()

    barrier = pltpu.get_barrier_semaphore()
    for d in range(1, ctx):
        pl.semaphore_signal(
            barrier, inc=1, device_id={"ctx": lax.rem(me + d, ctx)}, device_id_type=MESH
        )

    @pl.when(z > 0)
    def _():
        pl.semaphore_signal(barrier, inc=1, device_id={"head": z - 1}, device_id_type=MESH)

    @pl.when(z < heads - 1)
    def _():
        pl.semaphore_signal(barrier, inc=1, device_id={"head": z + 1}, device_id_type=MESH)

    for d in range(ctx):
        p, r = d // share, d % share
        cols = slice(r * qh * hd, (r + 1) * qh * hd)
        q_send[d, 0:span_dev] = queries_in[p * span_dev : (p + 1) * span_dev, cols]
        q_send[d, span_dev : span_dev + dec_dev] = queries_in[prompts * span_dev :, cols]
    base = 2 * prefix
    for p in range(prompts):
        for j in range(pages):
            slot = table[p, j]
            key_page = keys_in[slot]
            value_page = values_in[slot]
            for k in range(kvh):
                u = p * kvh + k
                kv_send[u, j * page : (j + 1) * page] = key_page[:, k * hd : (k + 1) * hd]
                kv_send[u, prefix + j * page : prefix + (j + 1) * page] = value_page[
                    :, k * hd : (k + 1) * hd
                ]
        for k in range(kvh):
            u = p * kvh + k
            mine = slice(p * span_dev, (p + 1) * span_dev)
            at = base
            for kind in range(2):
                kv_send[u, at : at + span_dev] = small_in[kind, mine, k * hd : (k + 1) * hd]
                at += span_dev
            for kind in range(2):
                kv_send[u, at : at + dec_dev] = small_in[
                    kind, prompts * span_dev :, k * hd : (k + 1) * hd
                ]
                at += dec_dev

    pl.semaphore_wait(
        barrier, ctx - 1 + jnp.where(z > 0, 1, 0) + jnp.where(z < heads - 1, 1, 0)
    )

    def unit_of(d):
        return d // share * kvh + d % share * kvh // share

    def send_queries(d):
        to = lax.rem(me + d, ctx)
        return remote(q_send.at[to], q_held.at[me], q_ssem.at[d], q_rsem.at[me], {"ctx": to})

    def send_keys(d):
        to = lax.rem(me + d, ctx)
        return remote(
            kv_send.at[unit_of(to)], kv_held.at[me], kv_ssem.at[d], kv_rsem.at[me], {"ctx": to}
        )

    for d in range(1, ctx):
        send_queries(d).start()
    for d in range(1, ctx):
        send_keys(d).start()
    own = (
        pltpu.make_async_copy(q_send.at[me], q_held.at[me], own_sem.at[0]),
        pltpu.make_async_copy(kv_send.at[unit_of(me)], kv_held.at[me], own_sem.at[1]),
    )
    for copy in own:
        copy.start()
    for copy in own:
        copy.wait()
    for d in range(1, ctx):
        at = lax.rem(me + d, ctx)
        remote(q_held.at[at], q_held.at[at], q_ssem.at[d], q_rsem.at[at], {"ctx": at}).wait_recv()
        remote(
            kv_held.at[at], kv_held.at[at], kv_ssem.at[d], kv_rsem.at[at], {"ctx": at}
        ).wait_recv()

    factor = math.log2(math.e) / math.sqrt(hd)
    at = base
    extra = []
    for width in (span_dev, span_dev, dec_dev, dec_dev):
        extra.append([kv_held[c, at : at + width] for c in range(ctx)])
        at += width
    extra_keys = jnp.concatenate(extra[0] + extra[2], axis=0)
    extra_values = jnp.concatenate(extra[1] + extra[3], axis=0)
    dq = jnp.concatenate([q_held[c, span_dev : span_dev + dec_dev] for c in range(ctx)], axis=0)
    dq = jnp.dot(pick_in[...], dq, preferred_element_type=F32).astype(BF16)
    sq = jnp.concatenate([q_held[c, 0:span_dev] for c in range(ctx)], axis=0)
    core_pair = me + 1 - 2 * lax.rem(me, 2)

    def far(e):
        return lax.rem(me + 2 * e, ctx)

    def to_sibling(b):
        return remote(
            attended.at[me, b], attended.at[me, b], sib_ssem.at[b], att_rsem.at[me, b], {"ctx": core_pair}
        )

    def to_far(e, b):
        return remote(
            attended.at[me, b], attended.at[me, b], far_ssem.at[e, b], att_rsem.at[me, b], {"ctx": far(e)}
        )

    def forward(e, b):
        s = far(e)
        return remote(
            attended.at[s, b], attended.at[s, b], fwd_ssem.at[e, b], att_rsem.at[s, b], {"ctx": core_pair}
        )

    def forward_all(b):
        for e in range(1, chips):
            forward(e, b).wait_recv()
            forward(e, b).start()

    def dot_keys(queries, keys):
        return lax.dot_general(queries, keys, (((1,), (1,)), ((), ())), preferred_element_type=F32)

    def attend(queries, bias):
        scores = [dot_keys(queries, kv_held[c, 0:prefix]) for c in range(ctx)]
        last = dot_keys(queries, extra_keys) + bias
        top = jnp.max(last, axis=1, keepdims=True)
        for s in scores:
            top = jnp.maximum(top, jnp.max(s, axis=1, keepdims=True))
        shift = top * factor
        w = jnp.exp2(last * factor - shift)
        total = jnp.sum(w, axis=1, keepdims=True)
        mixed = jnp.dot(w.astype(BF16), extra_values, preferred_element_type=F32)
        for c, s in enumerate(scores):
            w = jnp.exp2(s * factor - shift)
            total = total + jnp.sum(w, axis=1, keepdims=True)
            mixed = mixed + jnp.dot(
                w.astype(BF16), kv_held[c, prefix : 2 * prefix], preferred_element_type=F32
            )
        return (mixed / total).astype(BF16)

    def head_cols(rows, b, i):
        return rows[:, (b * pair + i) * hd : (b * pair + i + 1) * hd]

    for b in range(blocks):
        queries = jnp.concatenate(
            [head_cols(sq, b, i) for i in range(pair)] + [head_cols(dq, b, i) for i in range(pair)],
            axis=0,
        )
        bias = jnp.concatenate([bias_in[0:span]] * pair + [bias_in[span:]] * pair, axis=0)
        total_rows = queries.shape[0]
        slab = total_rows if total_rows <= 512 else 256
        mixed = jnp.concatenate(
            [attend(queries[s : s + slab], bias[s : s + slab]) for s in range(0, total_rows, slab)],
            axis=0,
        )
        for i in range(pair):
            attended[me, b, 0:span, i * hd : (i + 1) * hd] = mixed[i * span : (i + 1) * span]
            start = pair * span + i * picked
            attended[me, b, span : span + picked, i * hd : (i + 1) * hd] = mixed[
                start : start + picked
            ]
        to_sibling(b).start()
        for e in range(1, chips):
            to_far(e, b).start()
        if b > 0:
            forward_all(b - 1)
    forward_all(blocks - 1)

    for d in range(1, ctx):
        send_queries(d).wait_send()
        send_keys(d).wait_send()
    for b in range(blocks):
        to_sibling(b).wait_send()
        for e in range(1, chips):
            to_far(e, b).wait_send()
            forward(e, b).wait_send()
            s = lax.rem(core_pair + 2 * e, ctx)
            remote(
                attended.at[s, b], attended.at[s, b], fwd_ssem.at[e, b], att_rsem.at[s, b], {"ctx": core_pair}
            ).wait_recv()
        remote(
            attended.at[core_pair, b],
            attended.at[core_pair, b],
            sib_ssem.at[b],
            att_rsem.at[core_pair, b],
            {"ctx": core_pair},
        ).wait_recv()

    for d in range(ctx):
        p, r = d // share, d % share
        for b in range(blocks):
            cols = slice((r * qh + b * pair) * hd, (r * qh + (b + 1) * pair) * hd)
            rows_all[p * span : (p + 1) * span, cols] = attended[d, b, 0:span]
            decode_rows[p * picked : (p + 1) * picked, cols] = attended[d, b, span : span + picked]
    rows_all[prompts * span :] = jnp.dot(
        place_in[...], decode_rows[...], preferred_element_type=F32
    ).astype(BF16)

    def shift_right(g, o):
        return remote(
            right_out.at[g, o], right_in.at[g, o], right_ssem.at[g, o], right_rsem.at[g, o], {"head": z + 1}
        )

    def shift_left(g, o):
        return remote(
            left_out.at[g, o], left_in.at[g, o], left_ssem.at[g, o], left_rsem.at[g, o], {"head": z - 1}
        )

    def share_right(g, o):
        return remote(
            shared.at[g, o], shared.at[g, o], agr_ssem.at[g, o], ag_rsem.at[g, o], {"head": z + 1}
        )

    def share_left(g, o):
        return remote(
            shared.at[g, o], shared.at[g, o], agl_ssem.at[g, o], ag_rsem.at[g, o], {"head": z - 1}
        )

    def from_left(g, o):
        remote(
            right_out.at[g, o], right_in.at[g, o], right_ssem.at[g, o], right_rsem.at[g, o], {"head": z - 1}
        ).wait_recv()

    def from_right(g, o):
        remote(
            left_out.at[g, o], left_in.at[g, o], left_ssem.at[g, o], left_rsem.at[g, o], {"head": z + 1}
        ).wait_recv()

    def scatter(g):
        pltpu.make_async_copy(
            weight_in.at[:, g * gcols : (g + 1) * gcols], weight.at[g], weight_sem.at[g]
        ).wait()
        for o in range(heads):
            part[g, o] = jnp.dot(
                rows_all[o * srows : (o + 1) * srows], weight[g], preferred_element_type=F32
            )
        for k in range(heads - 1):
            o = heads - 1 - k

            @pl.when(z == 0)
            def _():
                right_out[g, o] = part[g, o].astype(BF16)
                shift_right(g, o).start()

            @pl.when((z > 0) & (z < o))
            def _():
                from_left(g, o)
                right_out[g, o] = (part[g, o] + right_in[g, o].astype(F32)).astype(BF16)
                shift_right(g, o).start()

            @pl.when(z == heads - 1)
            def _():
                left_out[g, k] = part[g, k].astype(BF16)
                shift_left(g, k).start()

            @pl.when((z < heads - 1) & (z > k))
            def _():
                from_right(g, k)
                left_out[g, k] = (part[g, k] + left_in[g, k].astype(F32)).astype(BF16)
                shift_left(g, k).start()

    def finish(g):
        @pl.when(z == 0)
        def _():
            from_right(g, 0)
            shared[g, 0] = (part[g, 0] + left_in[g, 0].astype(F32)).astype(BF16)
            share_right(g, 0).start()

        @pl.when(z == heads - 1)
        def _():
            o = heads - 1
            from_left(g, o)
            shared[g, o] = (part[g, o] + right_in[g, o].astype(F32)).astype(BF16)
            share_left(g, o).start()

        for o in range(1, heads - 1):

            @pl.when(z == o)
            def _():
                from_left(g, o)
                from_right(g, o)
                shared[g, o] = (
                    part[g, o] + right_in[g, o].astype(F32) + left_in[g, o].astype(F32)
                ).astype(BF16)
                share_right(g, o).start()
                share_left(g, o).start()

    def relay(g):
        for k in range(1, heads):

            @pl.when(z >= k)
            def _():
                o = z - k
                remote(
                    shared.at[g, o], shared.at[g, o], agr_ssem.at[g, o], ag_rsem.at[g, o], {"head": z - 1}
                ).wait_recv()

                @pl.when(z < heads - 1)
                def _():
                    share_right(g, o).start()

            @pl.when(z + k < heads)
            def _():
                o = z + k
                remote(
                    shared.at[g, o], shared.at[g, o], agl_ssem.at[g, o], ag_rsem.at[g, o], {"head": z + 1}
                ).wait_recv()

                @pl.when(z > 0)
                def _():
                    share_left(g, o).start()

        for o in range(heads):
            out_ref[o * srows : (o + 1) * srows, g * gcols : (g + 1) * gcols] = shared[g, o]

    for step in range(groups + 2):
        if step < groups:
            scatter(step)
        if 1 <= step <= groups:
            finish(step - 1)
        if step >= 2:
            relay(step - 2)

    for g in range(groups):
        for o in range(heads):

            @pl.when(z < o)
            def _():
                shift_right(g, o).wait_send()

            @pl.when(z > o)
            def _():
                shift_left(g, o).wait_send()

            @pl.when((o <= z) & (z < heads - 1))
            def _():
                share_right(g, o).wait_send()

            @pl.when((o >= z) & (z > 0))
            def _():
                share_left(g, o).wait_send()


def shards(
    ctx,
    heads,
    span_query,
    span_key,
    span_value,
    prefix_key,
    prefix_value,
    page_table,
    decode_query,
    decode_key,
    decode_value,
    sample_prompt,
    out_weight,
):
    prompts, span_dev, heads_dev, hd = span_query.shape
    kvh = span_key.shape[2]
    steps, samples_dev = decode_query.shape[:2]
    slots, page = prefix_key.shape[:2]
    pages = page_table.shape[1]
    samples = sample_prompt.shape[0]
    each = samples // prompts
    share = ctx // prompts
    qh = heads_dev // share
    pair = min(2, qh)
    dec_dev = steps * samples_dev
    span = ctx * span_dev
    picked = each * steps
    features, columns = out_weight.shape
    rows = prompts * span + steps * samples
    srows = rows // heads
    groups = 4
    gcols = columns // groups
    me = lax.axis_index("ctx")

    queries = jnp.concatenate(
        [
            span_query.reshape(prompts * span_dev, heads_dev * hd),
            decode_query.reshape(dec_dev, heads_dev * hd),
        ],
        axis=0,
    )
    small = jnp.stack(
        [
            jnp.concatenate(
                [s.reshape(prompts * span_dev, kvh * hd), d.reshape(dec_dev, kvh * hd)], axis=0
            )
            for s, d in ((span_key, decode_key), (span_value, decode_value))
        ]
    )
    keys = prefix_key.reshape(slots, page, kvh * hd)
    values = prefix_value.reshape(slots, page, kvh * hd)

    ids = jnp.arange(samples, dtype=jnp.int32)
    before = (ids[None, :] < ids[:, None]) & (sample_prompt[None, :] == sample_prompt[:, None])
    rank = jnp.sum(before.astype(jnp.int32), axis=1)
    chosen = (
        (rank[None, :] == jnp.arange(each, dtype=jnp.int32)[:, None])
        & (sample_prompt == me // share)[None, :]
    ).reshape(each, 1, ctx, 1, samples_dev)
    step_ids = jnp.arange(steps, dtype=jnp.int32)
    row_step = step_ids.reshape(1, steps, 1, 1, 1)
    col_step = step_ids.reshape(1, 1, 1, steps, 1)
    pick = (chosen & (row_step == col_step)).reshape(picked, ctx * dec_dev).astype(BF16)
    own = (chosen & (col_step <= row_step)).reshape(picked, ctx * dec_dev)
    pos = jnp.arange(span, dtype=jnp.int32)
    bias = jnp.concatenate(
        [
            jnp.concatenate(
                [pos[None, :] <= pos[:, None], jnp.zeros((span, ctx * dec_dev), bool)], axis=1
            ),
            jnp.concatenate([jnp.ones((picked, span), bool), own], axis=1),
        ],
        axis=0,
    )
    bias = jnp.where(bias, 0.0, masked_bias).astype(F32)
    target = (sample_prompt * picked + rank * steps)[None, :] + step_ids[:, None]
    place = (
        target.reshape(-1)[:, None] == jnp.arange(prompts * picked, dtype=jnp.int32)[None, :]
    ).astype(BF16)

    dims = (ctx, heads, prompts, kvh, pages, page, span_dev, dec_dev, qh, pair, picked, groups)
    blocks = qh // pair
    kv_rows = 2 * pages * page + 2 * span_dev + 2 * dec_dev
    vmem = pl.BlockSpec(memory_space=pltpu.VMEM)
    dma = pltpu.SemaphoreType.DMA
    sums = (groups, heads, srows, gcols)
    result = pl.pallas_call(
        functools.partial(kernel, dims),
        out_shape=jax.ShapeDtypeStruct((rows, columns), BF16),
        in_specs=[pl.BlockSpec(memory_space=pltpu.SMEM)]
        + [vmem] * 7
        + [pl.BlockSpec(memory_space=pl.ANY)],
        out_specs=vmem,
        scratch_shapes=[
            pltpu.VMEM((prompts * kvh, kv_rows, hd), BF16),
            pltpu.VMEM((ctx, span_dev + dec_dev, qh * hd), BF16),
            pltpu.VMEM((ctx, kv_rows, hd), BF16),
            pltpu.VMEM((ctx, span_dev + dec_dev, qh * hd), BF16),
            pltpu.VMEM((ctx, blocks, span + picked, pair * hd), BF16),
            pltpu.VMEM((rows, features), BF16),
            pltpu.VMEM((prompts * picked, features), BF16),
            pltpu.VMEM((groups, features, gcols), BF16),
            pltpu.VMEM(sums, F32),
            pltpu.VMEM(sums, BF16),
            pltpu.VMEM(sums, BF16),
            pltpu.VMEM(sums, BF16),
            pltpu.VMEM(sums, BF16),
            pltpu.VMEM(sums, BF16),
            dma((ctx,)),
            dma((ctx,)),
            dma((ctx,)),
            dma((ctx,)),
            dma((2,)),
            dma((blocks,)),
            dma((ctx // 2, blocks)),
            dma((ctx // 2, blocks)),
            dma((ctx, blocks)),
            dma((groups,)),
        ]
        + [dma((groups, heads))] * 7,
        compiler_params=pltpu.CompilerParams(
            collective_id=0, has_side_effects=True, vmem_limit_bytes=58 * 1024 * 1024
        ),
        cost_estimate=pl.CostEstimate(
            flops=2 * rows * features * columns, bytes_accessed=16 * 1024 * 1024, transcendentals=0
        ),
    )(page_table, keys, values, queries, small, bias, pick, place, out_weight)
    return (
        result[: prompts * span].reshape(prompts, span, columns),
        result[prompts * span :].reshape(steps, samples, columns),
    )


def solution(mesh):
    return jax.shard_map(
        functools.partial(shards, mesh.shape["ctx"], mesh.shape["head"]),
        mesh=mesh,
        in_specs=(
            P("groups", "ctx", "head", None),
            P("groups", "ctx", "head", None),
            P("groups", "ctx", "head", None),
            P(("groups", "ctx"), None, "head", None),
            P(("groups", "ctx"), None, "head", None),
            P("groups", "ctx"),
            P("groups", "ctx", "head", None),
            P("groups", "ctx", "head", None),
            P("groups", "ctx", "head", None),
            P("groups"),
            P("head", "ctx"),
        ),
        out_specs=(P("groups", None, "ctx"), P("groups", None, "ctx")),
        check_vma=False,
    )
```

time: 231 us -> 138 us (0.60)
  waiting for transfers between devices: 136 us -> 0 us
  Pallas kernels: 0 us -> 116 us
  matrix products: 30 us -> 0 us
  between operations: 14.1 us -> 0.68 us
  blocking collectives: 12.9 us -> 0 us
  other arithmetic: 16.2 us -> 5.39 us
  local copies, waits for them, and re-layouts: 20.6 us -> 14.8 us
    pallas_call x0 -> x1, Pallas kernels: none -> 116 us  [shards(): pl.pallas_call(functools.partial(kernel, dims), out_shape=jax.ShapeDtypeS...]
    all_gather x4 -> x0, waiting for transfers between devices: 75.4 us -> none  [the longest x1 37.3 us: shards(): summed = lax.all_gather(share, 'head', axis=0, tiled=True)]
    reduce_scatter x1 -> x0, waiting for transfers between devices: 60.4 us -> none  [shards(): lax.psum_scatter(projected, 'head', scatter_dimension=0, tiled=True)]
    dot_general x11 -> x0, matrix products: 30 us -> none  [the longest x4 10.4 us: absorb(): jnp.einsum('brn,bnd->brd', weights.astype(jnp.bfloat16), value_rows, pref...]
    all_gather x2 -> x0, blocking collectives: 12.9 us -> none  [the longest x1 6.69 us: shards(): lax.all_gather(span_key, 'ctx', axis=1, tiled=True)]
    reduce_sum x7 -> x1, other arithmetic: 8.51 us -> 0.91 us  [shards(): rank = jnp.sum(before.astype(jnp.int32), axis=1)]
    gather x2 -> x0, local copies, waits for them, and re-layouts: 4.24 us -> none  [the longest x1 2.64 us: shards(): jnp.take(prefix_value, slot_rows, axis=0)]
    reshape x8 -> x2, local copies, waits for them, and re-layouts: 7.35 us -> 4.33 us  [the longest x1 2.17 us: shards(): values = prefix_value.reshape(slots, page, kvh * hd)]
  transfers between devices with their start and end apart: 5 -> 0, of which waited for: 5 -> 0; matrix products, arithmetic and copies ran while one was open for 7% -> 0% of each run, Pallas kernels for 0% -> 0%
where the time goes in v1:
time: 138 us; the launch traced here: 137 us
  Pallas kernels  116 us (84%)
  local copies, waits for them, and re-layouts  14.8 us (11%)
  other arithmetic  5.39 us (4%)
    pallas_call x1, Pallas kernels, shards(): pl.pallas_call(functools.partial(kernel, dims), out_shape=jax.ShapeDtypeS...  116 us
    unnamed x6, local copies, waits for them, and re-layouts  4.93 us

profile of v1, /device:TPU:0, one launch (start us, length us, event | category | flops | bytes accessed | tf_op | source)
XLA Modules:
  0.0 137.3 jit_solution(7752809802136802675)
XLA Ops:
  0.6 0.7 broadcast_compare_fusion
  1.3 0.1 and.55
  1.4 0.9 convert_reduce_fusion
  2.3 0.7 multiply_add_fusion
  3.0 0.1 eq.66
  3.1 0.1 add.28
  3.2 0.7 copy.30
  3.9 0.7 copy.29
  4.6 0.7 fusion.3.place_in
  5.3 0.8 copy.28
  6.1 0.8 copy.27
  6.9 0.6 pad_maximum_fusion.1.small_in
  7.5 0.9 copy.26
  8.5 1.0 copy.25
  9.5 0.8 pad_maximum_fusion.queries_in
  10.3 0.3 and_convert_fusion
  10.6 0.8 reshape.129.pick_in
  11.4 0.3 and.61
  11.7 0.7 fusion.2.bias_in
  12.4 2.2 %reshape.119.keys_in = bf16[8,128,256]{2,1,0:T(8,128)(2,1)} reshape(bf16[8,128,2,128]{3,2,1,0:T(2,128)(2,1)} %param.14) | data formatting | bytes 1048576 | tf_op jit(solution)/shard_map/reshape | solution.py:480
  14.5 2.2 %reshape.120.values_in = bf16[8,128,256]{2,1,0:T(8,128)(2,1)} reshape(bf16[8,128,2,128]{3,2,1,0:T(2,128)(2,1)} %param.15) | data formatting | bytes 1048576 | tf_op jit(solution)/shard_map/reshape | solution.py:481
  16.7 116.4 %shard_map.122 = bf16[384,2048]{1,0:T(8,128)(2,1)} custom-call(s32[2,4]{1,0:T(2,128)} %table.1, bf16[8,128,256]{2,1,0:T(8,128)(2,1)} %reshape.119.keys_in, bf16[8,128,256]{2,1,0:T(8,128)(2,1)} %reshape.120.values_in, bf16[96,2048]{1,0:T(8,128)(2,1)} %pad_maximum_fusion.queries_in, bf16[2,96,256]{2,1,0:T(8,128)(2,1)} %pad_maximum_fusion.1.small_in, ...), custom_call_target="tpu_custom_call" | custom-call | flops 3221225472 | bytes 16777216 | tf_op jit(solution)/shard_map/pallas_call | solution.py:517
  133.1 1.9 %slice.7 = bf16[128,2048]{1,0:T(8,128)(2,1)} slice(bf16[384,2048]{1,0:T(8,128)(2,1)} %shard_map.122), slice={[256:384], [0:2048]} | slice | bytes 1048576 | tf_op jit(solution)/shard_map/slice | solution.py:560
  135.0 2.3 %slice.6 = bf16[256,2048]{1,0:T(8,128)(2,1)} slice(bf16[384,2048]{1,0:T(8,128)(2,1)} %shard_map.122), slice={[0:256], [0:2048]} | slice | bytes 2097152 | tf_op jit(solution)/shard_map/slice | solution.py:559
  (5 shorter events, 0.0 us)

commit v2 on v1

v2 whole, which is shorter than its diff:
```python
import functools
import math

import jax
import jax.numpy as jnp
from jax import lax
from jax.experimental import pallas as pl
from jax.experimental.pallas import tpu as pltpu
from jax.sharding import PartitionSpec as P

MESH = pl.DeviceIdType.MESH
F32 = jnp.float32
BF16 = jnp.bfloat16
masked_bias = -1e30


def div(x, n):
    if n & (n - 1):
        return x // n
    return lax.shift_right_logical(x, jnp.int32(n.bit_length() - 1))


def mod(x, n):
    if n & (n - 1):
        return x % n
    return x & (n - 1)


def iotas(rows, cols):
    shape = (rows, cols)
    return (
        lax.broadcasted_iota(jnp.int32, shape, 0),
        lax.broadcasted_iota(jnp.int32, shape, 1),
    )


def one_hot(mask):
    return jnp.where(mask, 1.0, 0.0).astype(BF16)


def exact(left, right):
    return jnp.dot(left, right, preferred_element_type=F32).astype(BF16)


def heads_first(outer, inner):
    i, j = iotas(outer * inner, outer * inner)
    return one_hot(j == mod(i, outer) * inner + div(i, outer))


def remote(src, dst, send, recv, device):
    return pltpu.make_async_remote_copy(
        src_ref=src,
        dst_ref=dst,
        send_sem=send,
        recv_sem=recv,
        device_id=device,
        device_id_type=MESH,
    )


def kernel(
    dims,
    table,
    prompt_in,
    keys_in,
    values_in,
    span_q_in,
    decode_q_in,
    span_k_in,
    span_v_in,
    decode_k_in,
    decode_v_in,
    weight_in,
    span_out,
    decode_out,
    kv_send,
    q_send,
    kv_held,
    q_held,
    attended,
    block_rows,
    weight,
    part,
    right_out,
    left_out,
    right_in,
    left_in,
    shared,
    summed,
    decode_rows,
    kv_ssem,
    kv_rsem,
    q_ssem,
    q_rsem,
    own_sem,
    sib_ssem,
    far_ssem,
    fwd_ssem,
    att_rsem,
    weight_sem,
    right_ssem,
    right_rsem,
    left_ssem,
    left_rsem,
    agr_ssem,
    agl_ssem,
    ag_rsem,
):
    (
        ctx,
        heads,
        prompts,
        kvh,
        heads_dev,
        pages,
        page,
        span_dev,
        steps,
        samples_dev,
        each,
        qh,
        nb,
        by_cols,
    ) = dims
    me = lax.axis_index("ctx")
    z = lax.axis_index("head")
    share = ctx // prompts
    hd = 128
    chips = ctx // 2
    prefix = pages * page
    dec_dev = steps * samples_dev
    samples = ctx * samples_dev
    span = ctx * span_dev
    picked = each * steps
    sb, pb = span // nb, picked // nb
    groups, unused, crows, ccols = shared.shape

    load_weight = pltpu.make_async_copy(weight_in, weight, weight_sem.at[0])
    load_weight.start()

    barrier = pltpu.get_barrier_semaphore()
    for d in range(1, ctx):
        pl.semaphore_signal(
            barrier, inc=1, device_id={"ctx": lax.rem(me + d, ctx)}, device_id_type=MESH
        )

    @pl.when(z > 0)
    def _():
        pl.semaphore_signal(barrier, inc=1, device_id={"head": z - 1}, device_id_type=MESH)

    @pl.when(z < heads - 1)
    def _():
        pl.semaphore_signal(barrier, inc=1, device_id={"head": z + 1}, device_id_type=MESH)

    order = heads_first(span_dev, heads_dev)
    block = span_dev * heads_dev
    span_rows = [
        exact(order, span_q_in[p * block : (p + 1) * block]) for p in range(prompts)
    ]
    dec_rows = exact(heads_first(dec_dev, heads_dev), decode_q_in[...])
    for d in range(ctx):
        p, r = d // share, d % share
        q_send[d, 0 : qh * span_dev] = span_rows[p][r * qh * span_dev : (r + 1) * qh * span_dev]
        q_send[d, qh * span_dev :] = dec_rows[r * qh * dec_dev : (r + 1) * qh * dec_dev]

    pl.semaphore_wait(
        barrier, ctx - 1 + jnp.where(z > 0, 1, 0) + jnp.where(z < heads - 1, 1, 0)
    )

    def unit_of(d):
        return d // share * kvh + d % share * kvh // share

    def send_queries(d):
        to = lax.rem(me + d, ctx)
        return remote(q_send.at[to], q_held.at[me], q_ssem.at[d], q_rsem.at[me], {"ctx": to})

    def send_keys(d):
        to = lax.rem(me + d, ctx)
        return remote(
            kv_send.at[unit_of(to)], kv_held.at[me], kv_ssem.at[d], kv_rsem.at[me], {"ctx": to}
        )

    for d in range(1, ctx):
        send_queries(d).start()

    def split(outer, keys, values):
        both = jnp.concatenate([keys, values], axis=1)
        if kvh == 1:
            return both
        return exact(heads_first(outer, kvh), both)

    base = 2 * prefix
    for p in range(prompts):
        for j in range(pages):
            slot = table[p, j]
            both = split(page, keys_in[slot], values_in[slot])
            for k in range(kvh):
                u = p * kvh + k
                rows = both[k * page : (k + 1) * page]
                kv_send[u, j * page : (j + 1) * page] = rows[:, :hd]
                kv_send[u, prefix + j * page : prefix + (j + 1) * page] = rows[:, hd:]
        size = span_dev * kvh
        mine = slice(p * size, (p + 1) * size)
        span_both = split(span_dev, span_k_in[mine], span_v_in[mine])
        dec_both = split(dec_dev, decode_k_in[...], decode_v_in[...])
        for k in range(kvh):
            u = p * kvh + k
            at = base
            for both, size in ((span_both, span_dev), (dec_both, dec_dev)):
                rows = both[k * size : (k + 1) * size]
                kv_send[u, at : at + size] = rows[:, :hd]
                kv_send[u, at + size : at + 2 * size] = rows[:, hd:]
                at += 2 * size

    for d in range(1, ctx):
        send_keys(d).start()
    own = (
        pltpu.make_async_copy(q_send.at[me], q_held.at[me], own_sem.at[0]),
        pltpu.make_async_copy(kv_send.at[unit_of(me)], kv_held.at[me], own_sem.at[1]),
    )
    for copy in own:
        copy.start()

    prompt_row = jnp.broadcast_to(prompt_in[...], (8, samples))
    i, j = iotas(samples, samples)
    earlier = one_hot(i < j)
    code = jnp.zeros((8, samples), F32)
    for p in range(prompts):
        here = one_hot(prompt_row == p)
        rank = jnp.dot(here, earlier, preferred_element_type=F32)
        code = code + here.astype(F32) * (rank + p * each)
    code = code.astype(BF16)

    i, j = iotas(samples, ctx * dec_dev)
    spread = one_hot(i == div(j, dec_dev) * samples_dev + mod(j, samples_dev))
    col_code = jnp.dot(code, spread, preferred_element_type=F32)[0:1]
    i, j = iotas(picked, ctx * dec_dev)
    wanted = (div(i, steps) + me // share * each).astype(F32)
    same = jnp.where(col_code == wanted, 1, 0)
    later = mod(i, steps) - mod(div(j, samples_dev), steps)
    pick = one_hot((same == 1) & (later == 0))
    own_bias = jnp.where((same == 1) & (later >= 0), 0.0, masked_bias)
    i, j = iotas(span, span)
    span_bias = jnp.where(j <= i, 0.0, masked_bias)

    for copy in own:
        copy.wait()
    for d in range(1, ctx):
        at = lax.rem(me + d, ctx)
        remote(q_held.at[at], q_held.at[at], q_ssem.at[d], q_rsem.at[at], {"ctx": at}).wait_recv()
    dq = jnp.concatenate(
        [
            jnp.concatenate(
                [
                    q_held[c, qh * span_dev + g * dec_dev : qh * span_dev + (g + 1) * dec_dev]
                    for c in range(ctx)
                ],
                axis=0,
            )
            for g in range(qh)
        ],
        axis=1,
    )
    dq = exact(pick, dq)
    for d in range(1, ctx):
        at = lax.rem(me + d, ctx)
        remote(
            kv_held.at[at], kv_held.at[at], kv_ssem.at[d], kv_rsem.at[at], {"ctx": at}
        ).wait_recv()

    factor = math.log2(math.e) / math.sqrt(hd)
    at = base
    extra = []
    for width in (span_dev, span_dev, dec_dev, dec_dev):
        extra.append([kv_held[c, at : at + width] for c in range(ctx)])
        at += width
    extra_keys = jnp.concatenate(extra[0] + extra[2], axis=0)
    extra_values = jnp.concatenate(extra[1] + extra[3], axis=0)
    core_pair = me + 1 - 2 * lax.rem(me, 2)

    def far(e):
        return lax.rem(me + 2 * e, ctx)

    def gather_copy(source, b, sem, to):
        rows = attended.at[source, b]
        return remote(rows, rows, sem, att_rsem.at[source, b], {"ctx": to})

    def to_sibling(b):
        return gather_copy(me, b, sib_ssem.at[b], core_pair)

    def to_far(e, b):
        return gather_copy(me, b, far_ssem.at[e, b], far(e))

    def forward(e, b):
        return gather_copy(far(e), b, fwd_ssem.at[e, b], core_pair)

    def forward_all(b):
        for e in range(1, chips):
            forward(e, b).wait_recv()
            forward(e, b).start()

    def dot_keys(queries, keys):
        return lax.dot_general(queries, keys, (((1,), (1,)), ((), ())), preferred_element_type=F32)

    def attend(queries, bias):
        scores = [dot_keys(queries, kv_held[c, 0:prefix]) for c in range(ctx)]
        last = dot_keys(queries, extra_keys) + bias
        top = jnp.max(last, axis=1, keepdims=True)
        for s in scores:
            top = jnp.maximum(top, jnp.max(s, axis=1, keepdims=True))
        shift = top * factor
        w = jnp.exp2(last * factor - shift)
        total = jnp.sum(w, axis=1, keepdims=True)
        mixed = jnp.dot(w.astype(BF16), extra_values, preferred_element_type=F32)
        for c, s in enumerate(scores):
            w = jnp.exp2(s * factor - shift)
            total = total + jnp.sum(w, axis=1, keepdims=True)
            mixed = mixed + jnp.dot(
                w.astype(BF16), kv_held[c, prefix : 2 * prefix], preferred_element_type=F32
            )
        return (mixed / total).astype(BF16)

    per_block = ctx // nb

    def attend_half(b, half):
        split_at = (qh + 1) // 2
        chosen = range(0, split_at) if half == 0 else range(split_at, qh)
        count = len(chosen)
        if count == 0:
            return
        sources = range(b * per_block, (b + 1) * per_block)
        queries = [
            q_held[c, g * span_dev : (g + 1) * span_dev] for g in chosen for c in sources
        ] + [dq[b * pb : (b + 1) * pb, g * hd : (g + 1) * hd] for g in chosen]
        span_part = jnp.concatenate(
            [span_bias[b * sb : (b + 1) * sb], jnp.full((sb, ctx * dec_dev), masked_bias, F32)],
            axis=1,
        )
        dec_part = jnp.concatenate(
            [jnp.zeros((pb, span), F32), own_bias[b * pb : (b + 1) * pb]], axis=1
        )
        bias = jnp.concatenate([span_part] * count + [dec_part] * count, axis=0)
        mixed = attend(jnp.concatenate(queries, axis=0), bias)
        for n, g in enumerate(chosen):
            cols = slice(g * hd, (g + 1) * hd)
            attended[me, b, 0:sb, cols] = mixed[n * sb : (n + 1) * sb]
            start = count * sb + n * pb
            attended[me, b, sb : sb + pb, cols] = mixed[start : start + pb]

    def collect(b):
        gather_copy(core_pair, b, sib_ssem.at[b], core_pair).wait_recv()
        for e in range(1, chips):
            gather_copy(
                lax.rem(core_pair + 2 * e, ctx), b, fwd_ssem.at[e, b], core_pair
            ).wait_recv()
        for d in range(ctx):
            p, r = d // share, d % share
            cols = slice(r * qh * hd, (r + 1) * qh * hd)
            block_rows[b, p * sb : (p + 1) * sb, cols] = attended[d, b, 0:sb]
            start = prompts * sb + p * pb
            block_rows[b, start : start + pb, cols] = attended[d, b, sb : sb + pb]

    def piece(g, o):
        b, half = g // 2, g % 2
        row = 0 if by_cols else o * crows
        col = (2 * o + half if by_cols else half) * ccols
        return b, slice(row, row + crows), slice(col, col + ccols)

    def shift_right(g, o, to):
        return remote(
            right_out.at[g, o], right_in.at[g, o], right_ssem.at[g, o], right_rsem.at[g, o], {"head": to}
        )

    def shift_left(g, o, to):
        return remote(
            left_out.at[g, o], left_in.at[g, o], left_ssem.at[g, o], left_rsem.at[g, o], {"head": to}
        )

    def share_right(g, o, to):
        rows = shared.at[g, o]
        return remote(rows, rows, agr_ssem.at[g, o], ag_rsem.at[g, o], {"head": to})

    def share_left(g, o, to):
        rows = shared.at[g, o]
        return remote(rows, rows, agl_ssem.at[g, o], ag_rsem.at[g, o], {"head": to})

    def when_group(g):
        return pl.when((g >= 0) & (g < groups))

    def project(g):
        for o in range(heads):
            b, rows, cols = piece(g, o)
            part[g, o] = jnp.dot(
                block_rows[b, rows], weight[:, cols], preferred_element_type=F32
            )

    def hop(tick):
        g = tick - z

        @when_group(g)
        def _():
            for o in range(heads - 1, 0, -1):

                @pl.when(z == 0)
                def _():
                    right_out[g, o] = part[g, o].astype(BF16)
                    shift_right(g, o, z + 1).start()

                @pl.when((z > 0) & (z < o))
                def _():
                    shift_right(g, o, z - 1).wait_recv()
                    right_out[g, o] = (part[g, o] + right_in[g, o].astype(F32)).astype(BF16)
                    shift_right(g, o, z + 1).start()

        h = tick - (heads - 1 - z)

        @when_group(h)
        def _():
            for o in range(heads - 1):

                @pl.when(z == heads - 1)
                def _():
                    left_out[h, o] = part[h, o].astype(BF16)
                    shift_left(h, o, z - 1).start()

                @pl.when((z < heads - 1) & (z > o))
                def _():
                    shift_left(h, o, z + 1).wait_recv()
                    left_out[h, o] = (part[h, o] + left_in[h, o].astype(F32)).astype(BF16)
                    shift_left(h, o, z - 1).start()

    def ready(o):
        return jnp.maximum(o, heads - 1 - o)

    def finish(tick):
        g = tick - ready(z)

        @when_group(g)
        def _():
            @pl.when(z == 0)
            def _():
                shift_left(g, z, z + 1).wait_recv()
                shared[g, z] = (part[g, z] + left_in[g, z].astype(F32)).astype(BF16)
                share_right(g, z, z + 1).start()

            @pl.when(z == heads - 1)
            def _():
                shift_right(g, z, z - 1).wait_recv()
                shared[g, z] = (part[g, z] + right_in[g, z].astype(F32)).astype(BF16)
                share_left(g, z, z - 1).start()

            @pl.when((z > 0) & (z < heads - 1))
            def _():
                shift_right(g, z, z - 1).wait_recv()
                shift_left(g, z, z + 1).wait_recv()
                shared[g, z] = (
                    part[g, z] + right_in[g, z].astype(F32) + left_in[g, z].astype(F32)
                ).astype(BF16)
                share_right(g, z, z + 1).start()
                share_left(g, z, z - 1).start()

    def relay(tick):
        for k in range(1, heads):
            o = z - k
            g = tick - ready(o) - k

            @pl.when((o >= 0) & (g >= 0) & (g < groups))
            def _():
                share_right(g, o, z - 1).wait_recv()

                @pl.when(z < heads - 1)
                def _():
                    share_right(g, o, z + 1).start()

            q = z + k
            h = tick - ready(q) - k

            @pl.when((q < heads) & (h >= 0) & (h < groups))
            def _():
                share_left(h, q, z + 1).wait_recv()

                @pl.when(z > 0)
                def _():
                    share_left(h, q, z - 1).start()

    def tick(t):
        if t < groups:
            project(t)
        hop(t)
        finish(t)
        relay(t)

    for b in range(nb):
        attend_half(b, 0)
        if b == 0:
            load_weight.wait()
        if b >= 1:
            forward_all(b - 1)
        if b >= 2:
            tick(2 * (b - 2) + 1)
        attend_half(b, 1)
        to_sibling(b).start()
        for e in range(1, chips):
            to_far(e, b).start()
        if b >= 1:
            collect(b - 1)
            tick(2 * (b - 1))
    forward_all(nb - 1)
    tick(2 * (nb - 2) + 1)
    collect(nb - 1)
    for t in range(2 * (nb - 1), groups + 2 * (heads - 1)):
        tick(t)

    for g in range(groups):
        for o in range(heads):
            b, rows, cols = piece(g, o)
            summed[b, rows, cols] = shared[g, o]
    for b in range(nb):
        for p in range(prompts):
            span_out[p * span + b * sb : p * span + (b + 1) * sb] = summed[b, p * sb : (p + 1) * sb]
            start = prompts * sb + p * pb
            decode_rows[p * picked + b * pb : p * picked + (b + 1) * pb] = summed[
                b, start : start + pb
            ]
    i, j = iotas(samples, steps * samples)
    col_code = jnp.dot(code, one_hot(i == mod(j, samples)), preferred_element_type=F32)[0:1]
    i, j = iotas(prompts * picked, steps * samples)
    same = jnp.where(col_code == div(i, steps).astype(F32), 1, 0)
    place = one_hot((same == 1) & (div(j, samples) == mod(i, steps)))
    decode_out[...] = lax.dot_general(
        place, decode_rows[...], (((0,), (0,)), ((), ())), preferred_element_type=F32
    ).astype(BF16)

    for d in range(1, ctx):
        send_queries(d).wait_send()
        send_keys(d).wait_send()
    for b in range(nb):
        to_sibling(b).wait_send()
        for e in range(1, chips):
            to_far(e, b).wait_send()
            forward(e, b).wait_send()
    for g in range(groups):
        for o in range(heads):

            @pl.when(z < o)
            def _():
                shift_right(g, o, z + 1).wait_send()

            @pl.when(z > o)
            def _():
                shift_left(g, o, z - 1).wait_send()

            @pl.when((o <= z) & (z < heads - 1))
            def _():
                share_right(g, o, z + 1).wait_send()

            @pl.when((o >= z) & (z > 0))
            def _():
                share_left(g, o, z - 1).wait_send()


def shards(
    ctx,
    heads,
    span_query,
    span_key,
    span_value,
    prefix_key,
    prefix_value,
    page_table,
    decode_query,
    decode_key,
    decode_value,
    sample_prompt,
    out_weight,
):
    prompts, span_dev, heads_dev, hd = span_query.shape
    kvh = span_key.shape[2]
    steps, samples_dev = decode_query.shape[:2]
    slots, page = prefix_key.shape[:2]
    pages = page_table.shape[1]
    samples = sample_prompt.shape[0]
    each = samples // prompts
    qh = heads_dev * prompts // ctx
    dec_dev = steps * samples_dev
    span = ctx * span_dev
    picked = each * steps
    features, columns = out_weight.shape
    nb = 4
    groups = 2 * nb
    brows = (prompts * span + steps * samples) // nb
    by_cols = columns // heads >= 256
    crows = brows if by_cols else brows // heads
    ccols = (columns // heads if by_cols else columns) // 2

    dims = (
        ctx,
        heads,
        prompts,
        kvh,
        heads_dev,
        pages,
        page,
        span_dev,
        steps,
        samples_dev,
        each,
        qh,
        nb,
        by_cols,
    )
    kv_rows = 2 * pages * page + 2 * span_dev + 2 * dec_dev
    q_rows = qh * (span_dev + dec_dev)
    vmem = pl.BlockSpec(memory_space=pltpu.VMEM)
    dma = pltpu.SemaphoreType.DMA
    sums = (groups, heads, crows, ccols)
    span_out, decode_out = pl.pallas_call(
        functools.partial(kernel, dims),
        out_shape=(
            jax.ShapeDtypeStruct((prompts * span, columns), BF16),
            jax.ShapeDtypeStruct((steps * samples, columns), BF16),
        ),
        in_specs=[pl.BlockSpec(memory_space=pltpu.SMEM)]
        + [vmem] * 9
        + [pl.BlockSpec(memory_space=pl.ANY)],
        out_specs=(vmem, vmem),
        scratch_shapes=[
            pltpu.VMEM((prompts * kvh, kv_rows, hd), BF16),
            pltpu.VMEM((ctx, q_rows, hd), BF16),
            pltpu.VMEM((ctx, kv_rows, hd), BF16),
            pltpu.VMEM((ctx, q_rows, hd), BF16),
            pltpu.VMEM((ctx, nb, (span + picked) // nb, qh * hd), BF16),
            pltpu.VMEM((nb, brows, features), BF16),
            pltpu.VMEM((features, columns), BF16),
            pltpu.VMEM(sums, F32),
            pltpu.VMEM(sums, BF16),
            pltpu.VMEM(sums, BF16),
            pltpu.VMEM(sums, BF16),
            pltpu.VMEM(sums, BF16),
            pltpu.VMEM(sums, BF16),
            pltpu.VMEM((nb, brows, columns), BF16),
            pltpu.VMEM((prompts * picked, columns), BF16),
            dma((ctx,)),
            dma((ctx,)),
            dma((ctx,)),
            dma((ctx,)),
            dma((2,)),
            dma((nb,)),
            dma((ctx // 2, nb)),
            dma((ctx // 2, nb)),
            dma((ctx, nb)),
            dma((1,)),
        ]
        + [dma((groups, heads))] * 7,
        compiler_params=pltpu.CompilerParams(
            collective_id=0, has_side_effects=True, vmem_limit_bytes=58 * 1024 * 1024
        ),
        cost_estimate=pl.CostEstimate(
            flops=2 * prompts * span * features * columns,
            bytes_accessed=16 * 1024 * 1024,
            transcendentals=0,
        ),
    )(
        page_table,
        sample_prompt.reshape(1, samples),
        prefix_key.reshape(slots, page * kvh, hd),
        prefix_value.reshape(slots, page * kvh, hd),
        span_query.reshape(-1, hd),
        decode_query.reshape(-1, hd),
        span_key.reshape(-1, hd),
        span_value.reshape(-1, hd),
        decode_key.reshape(-1, hd),
        decode_value.reshape(-1, hd),
        out_weight,
    )
    return (
        span_out.reshape(prompts, span, columns),
        decode_out.reshape(steps, samples, columns),
    )


def solution(mesh):
    return jax.shard_map(
        functools.partial(shards, mesh.shape["ctx"], mesh.shape["head"]),
        mesh=mesh,
        in_specs=(
            P("groups", "ctx", "head", None),
            P("groups", "ctx", "head", None),
            P("groups", "ctx", "head", None),
            P(("groups", "ctx"), None, "head", None),
            P(("groups", "ctx"), None, "head", None),
            P("groups", "ctx"),
            P("groups", "ctx", "head", None),
            P("groups", "ctx", "head", None),
            P("groups", "ctx", "head", None),
            P("groups"),
            P("head", "ctx"),
        ),
        out_specs=(P("groups", None, "ctx"), P("groups", None, "ctx")),
        check_vma=False,
    )
```

time: 138 us -> 89.3 us (0.65)
  Pallas kernels: 116 us -> 84.2 us
  local copies, waits for them, and re-layouts: 14.8 us -> 4.18 us
  other arithmetic: 5.39 us -> 0 us
    pallas_call x1, Pallas kernels: 116 us -> 84.2 us  [shards(): pl.pallas_call(functools.partial(kernel, dims), out_shape=(jax.ShapeDtype...]
    reshape x2 -> x0, local copies, waits for them, and re-layouts: 4.33 us -> none  [the longest x1 2.17 us: shards(): values = prefix_value.reshape(slots, page, kvh * hd)]
    slice x2 -> x0, local copies, waits for them, and re-layouts: 4.19 us -> none  [the longest x1 2.3 us: shards(): result[:prompts * span].reshape(prompts, span, columns)]
    unnamed x6 -> x2, local copies, waits for them, and re-layouts: 4.93 us -> 4.18 us
where the time goes in v2:
time: 89.3 us; the launch traced here: 89 us
  Pallas kernels  84.2 us (94%)
  local copies, waits for them, and re-layouts  4.18 us (5%)
    pallas_call x1, Pallas kernels, shards(): pl.pallas_call(functools.partial(kernel, dims), out_shape=(jax.ShapeDtype...  84.2 us
    unnamed x2, local copies, waits for them, and re-layouts  4.18 us

profile of v2, /device:TPU:0, one launch (start us, length us, event | category | flops | bytes accessed | tf_op | source)
XLA Modules:
  0.0 89.0 jit_solution(13860663442823514095)
XLA Ops:
  0.6 84.2 %shard_map.122 = (bf16[256,2048]{1,0:T(8,128)(2,1)}, bf16[128,2048]{1,0:T(8,128)(2,1)}) custom-call(s32[2,4]{1,0:T(2,128)} %table.1, s32[1,32]{1,0:T(1,128)} %bitcast.21, bf16[8,256,128]{2,1,0:T(8,128)(2,1)} %bitcast.13, bf16[8,256,128]{2,1,0:T(8,128)(2,1)} %bitcast.14, bf16[1024,128]{1,0:T(8,128)(2,1)} %bitcast.15, bf16[512,128]{1,0:T(8,128)(2,1)} %bitcast.16, ...), custom_call_target="tpu_custom_call" | custom-call | flops 2147483648 | bytes 16777216 | tf_op jit(solution)/shard_map/pallas_call | solution.py:617
  84.8 2.3 %copy.15 = bf16[2,128,2048]{2,1,0:T(8,128)(2,1)} copy(bf16[2,128,2048]{2,1,0:T(8,128)(2,1)} %bitcast.11) | data formatting | bytes 2097152
  87.1 1.9 %copy.16 = bf16[4,32,2048]{2,1,0:T(8,128)(2,1)} copy(bf16[4,32,2048]{2,1,0:T(8,128)(2,1)} %bitcast.12) | data formatting | bytes 1048576

commit v3 on v2

--- a/solution.py
+++ b/solution.py
@@ -71,8 +71,8 @@
     decode_k_in,
     decode_v_in,
     weight_in,
-    span_out,
-    decode_out,
+    summed,
+    place_out,
     kv_send,
     q_send,
     kv_held,
@@ -86,12 +86,12 @@
     right_in,
     left_in,
     shared,
-    summed,
-    decode_rows,
     kv_ssem,
     kv_rsem,
     q_ssem,
     q_rsem,
+    s_ssem,
+    s_rsem,
     own_sem,
     sib_ssem,
     far_ssem,
@@ -105,6 +105,7 @@
     agr_ssem,
     agl_ssem,
     ag_rsem,
+    done_sem,
 ):
     (
         ctx,
@@ -170,9 +171,21 @@
     def unit_of(d):
         return d // share * kvh + d % share * kvh // share
 
+    core_pair = me + 1 - 2 * lax.rem(me, 2)
+    q_span = pl.ds(0, qh * span_dev)
+    q_dec = pl.ds(qh * span_dev, qh * dec_dev)
+
     def send_queries(d):
         to = lax.rem(me + d, ctx)
-        return remote(q_send.at[to], q_held.at[me], q_ssem.at[d], q_rsem.at[me], {"ctx": to})
+        return remote(
+            q_send.at[to, q_dec], q_held.at[me, q_dec], q_ssem.at[d], q_rsem.at[me], {"ctx": to}
+        )
+
+    def send_span(d):
+        to = lax.rem(me + d, ctx)
+        return remote(
+            q_send.at[to, q_span], q_held.at[me, q_span], s_ssem.at[d], s_rsem.at[me], {"ctx": to}
+        )
 
     def send_keys(d):
         to = lax.rem(me + d, ctx)
@@ -182,6 +195,10 @@
 
     for d in range(1, ctx):
         send_queries(d).start()
+
+        @pl.when(lax.rem(me + d, ctx) == core_pair)
+        def _():
+            send_span(d).start()
 
     def split(outer, keys, values):
         both = jnp.concatenate([keys, values], axis=1)
@@ -240,14 +257,19 @@
     later = mod(i, steps) - mod(div(j, samples_dev), steps)
     pick = one_hot((same == 1) & (later == 0))
     own_bias = jnp.where((same == 1) & (later >= 0), 0.0, masked_bias)
-    i, j = iotas(span, span)
-    span_bias = jnp.where(j <= i, 0.0, masked_bias)
+
+    i, j = iotas(samples, steps * samples)
+    col_code = jnp.dot(code, one_hot(i == mod(j, samples)), preferred_element_type=F32)[0:1]
+    i, j = iotas(prompts * picked, steps * samples)
+    same = jnp.where(col_code == div(i, steps).astype(F32), 1, 0)
+    place_out[...] = one_hot((same == 1) & (div(j, samples) == mod(i, steps)))
 
     for copy in own:
         copy.wait()
     for d in range(1, ctx):
         at = lax.rem(me + d, ctx)
-        remote(q_held.at[at], q_held.at[at], q_ssem.at[d], q_rsem.at[at], {"ctx": at}).wait_recv()
+        rows = q_held.at[at, q_dec]
+        remote(rows, rows, q_ssem.at[d], q_rsem.at[at], {"ctx": at}).wait_recv()
     dq = jnp.concatenate(
         [
             jnp.concatenate(
@@ -267,6 +289,11 @@
         remote(
             kv_held.at[at], kv_held.at[at], kv_ssem.at[d], kv_rsem.at[at], {"ctx": at}
         ).wait_recv()
+    for d in range(1, ctx):
+
+        @pl.when(lax.rem(me + d, ctx) != core_pair)
+        def _():
+            send_span(d).start()
 
     factor = math.log2(math.e) / math.sqrt(hd)
     at = base
@@ -276,7 +303,6 @@
         at += width
     extra_keys = jnp.concatenate(extra[0] + extra[2], axis=0)
     extra_values = jnp.concatenate(extra[1] + extra[3], axis=0)
-    core_pair = me + 1 - 2 * lax.rem(me, 2)
 
     def far(e):
         return lax.rem(me + 2 * e, ctx)
@@ -328,13 +354,33 @@
         count = len(chosen)
         if count == 0:
             return
-        sources = range(b * per_block, (b + 1) * per_block)
+        sources = [
+            lax.rem(me // share * share + b * per_block + n, ctx) for n in range(per_block)
+        ]
+        if half == 0:
+            for c in sources:
+
+                @pl.when(c != me)
+                def _():
+                    rows = q_held.at[c, q_span]
+                    remote(rows, rows, s_ssem.at[0], s_rsem.at[c], {"ctx": c}).wait_recv()
+
         queries = [
             q_held[c, g * span_dev : (g + 1) * span_dev] for g in chosen for c in sources
         ] + [dq[b * pb : (b + 1) * pb, g * hd : (g + 1) * hd] for g in chosen]
+        i, j = iotas(span_dev, span)
         span_part = jnp.concatenate(
-            [span_bias[b * sb : (b + 1) * sb], jnp.full((sb, ctx * dec_dev), masked_bias, F32)],
-            axis=1,
+            [
+                jnp.concatenate(
+                    [
+                        jnp.where(j <= i + c * span_dev, 0.0, masked_bias),
+                        jnp.full((span_dev, ctx * dec_dev), masked_bias, F32),
+                    ],
+                    axis=1,
+                )
+                for c in sources
+            ],
+            axis=0,
         )
         dec_part = jnp.concatenate(
             [jnp.zeros((pb, span), F32), own_bias[b * pb : (b + 1) * pb]], axis=1
@@ -483,12 +529,22 @@
                 def _():
                     share_left(h, q, z - 1).start()
 
+    def store(g, o):
+        b, rows, cols = piece(g, o)
+        return pltpu.make_async_copy(
+            shared.at[g, o], summed.at[b, rows, cols], done_sem.at[g, o]
+        )
+
     def tick(t):
         if t < groups:
             project(t)
         hop(t)
         finish(t)
         relay(t)
+        g = t - 2 * (heads - 1)
+        if g >= 0:
+            for o in range(heads):
+                store(g, o).start()
 
     for b in range(nb):
         attend_half(b, 0)
@@ -511,28 +567,9 @@
     for t in range(2 * (nb - 1), groups + 2 * (heads - 1)):
         tick(t)
 
-    for g in range(groups):
-        for o in range(heads):
-            b, rows, cols = piece(g, o)
-            summed[b, rows, cols] = shared[g, o]
-    for b in range(nb):
-        for p in range(prompts):
-            span_out[p * span + b * sb : p * span + (b + 1) * sb] = summed[b, p * sb : (p + 1) * sb]
-            start = prompts * sb + p * pb
-            decode_rows[p * picked + b * pb : p * picked + (b + 1) * pb] = summed[
-                b, start : start + pb
-            ]
-    i, j = iotas(samples, steps * samples)
-    col_code = jnp.dot(code, one_hot(i == mod(j, samples)), preferred_element_type=F32)[0:1]
-    i, j = iotas(prompts * picked, steps * samples)
-    same = jnp.where(col_code == div(i, steps).astype(F32), 1, 0)
-    place = one_hot((same == 1) & (div(j, samples) == mod(i, steps)))
-    decode_out[...] = lax.dot_general(
-        place, decode_rows[...], (((0,), (0,)), ((), ())), preferred_element_type=F32
-    ).astype(BF16)
-
     for d in range(1, ctx):
         send_queries(d).wait_send()
+        send_span(d).wait_send()
         send_keys(d).wait_send()
     for b in range(nb):
         to_sibling(b).wait_send()
@@ -557,6 +594,26 @@
             @pl.when((o >= z) & (z > 0))
             def _():
                 share_left(g, o, z - 1).wait_send()
+
+            store(g, o).wait()
+
+
+def place_rows(dims, place, summed, span_out, decode_out, decode_rows):
+    prompts, share, per_block, ctx, span_dev, sb, pb, picked, nb = dims
+    span = ctx * span_dev
+    for b in range(nb):
+        for p in range(prompts):
+            for n in range(per_block):
+                c = (p * share + b * per_block + n) % ctx
+                to = p * span + c * span_dev
+                start = p * sb + n * span_dev
+                span_out[to : to + span_dev] = summed[b, start : start + span_dev]
+            start = prompts * sb + p * pb
+            to = p * picked + b * pb
+            decode_rows[to : to + pb] = summed[b, start : start + pb]
+    decode_out[...] = lax.dot_general(
+        place[...], decode_rows[...], (((0,), (0,)), ((), ())), preferred_element_type=F32
+    ).astype(BF16)
 
 
 def shards(
@@ -614,16 +671,16 @@
     vmem = pl.BlockSpec(memory_space=pltpu.VMEM)
     dma = pltpu.SemaphoreType.DMA
     sums = (groups, heads, crows, ccols)
-    span_out, decode_out = pl.pallas_call(
+    summed, place = pl.pallas_call(
         functools.partial(kernel, dims),
         out_shape=(
-            jax.ShapeDtypeStruct((prompts * span, columns), BF16),
-            jax.ShapeDtypeStruct((steps * samples, columns), BF16),
+            jax.ShapeDtypeStruct((nb, brows, columns), BF16),
+            jax.ShapeDtypeStruct((prompts * picked, steps * samples), BF16),
         ),
         in_specs=[pl.BlockSpec(memory_space=pltpu.SMEM)]
         + [vmem] * 9
         + [pl.BlockSpec(memory_space=pl.ANY)],
-        out_specs=(vmem, vmem),
+        out_specs=(pl.BlockSpec(memory_space=pl.ANY), vmem),
         scratch_shapes=[
             pltpu.VMEM((prompts * kvh, kv_rows, hd), BF16),
             pltpu.VMEM((ctx, q_rows, hd), BF16),
@@ -638,8 +695,8 @@
             pltpu.VMEM(sums, BF16),
             pltpu.VMEM(sums, BF16),
             pltpu.VMEM(sums, BF16),
-            pltpu.VMEM((nb, brows, columns), BF16),
-            pltpu.VMEM((prompts * picked, columns), BF16),
+            dma((ctx,)),
+            dma((ctx,)),
             dma((ctx,)),
             dma((ctx,)),
             dma((ctx,)),
@@ -651,7 +708,7 @@
             dma((ctx, nb)),
             dma((1,)),
         ]
-        + [dma((groups, heads))] * 7,
+        + [dma((groups, heads))] * 8,
         compiler_params=pltpu.CompilerParams(
             collective_id=0, has_side_effects=True, vmem_limit_bytes=58 * 1024 * 1024
         ),
@@ -673,6 +730,41 @@
         decode_value.reshape(-1, hd),
         out_weight,
     )
+    width = math.gcd(columns, 512)
+    place_dims = (
+        prompts,
+        ctx // prompts,
+        ctx // nb,
+        ctx,
+        span_dev,
+        span // nb,
+        picked // nb,
+        picked,
+        nb,
+    )
+    span_out, decode_out = pl.pallas_call(
+        functools.partial(place_rows, place_dims),
+        grid=(columns // width,),
+        out_shape=(
+            jax.ShapeDtypeStruct((prompts * span, columns), BF16),
+            jax.ShapeDtypeStruct((steps * samples, columns), BF16),
+        ),
+        in_specs=[
+            pl.BlockSpec((prompts * picked, steps * samples), lambda i: (0, 0)),
+            pl.BlockSpec((nb, brows, width), lambda i: (0, 0, i)),
+        ],
+        out_specs=(
+            pl.BlockSpec((prompts * span, width), lambda i: (0, i)),
+            pl.BlockSpec((steps * samples, width), lambda i: (0, i)),
+        ),
+        scratch_shapes=[pltpu.VMEM((prompts * picked, width), BF16)],
+        compiler_params=pltpu.CompilerParams(vmem_limit_bytes=58 * 1024 * 1024),
+        cost_estimate=pl.CostEstimate(
+            flops=2 * (steps * samples) ** 2 * columns,
+            bytes_accessed=4 * brows * nb * columns,
+            transcendentals=0,
+        ),
+    )(place, summed)
     return (
         span_out.reshape(prompts, span, columns),
         decode_out.reshape(steps, samples, columns),

time: 89.3 us -> 85.9 us (0.962)
  local copies, waits for them, and re-layouts: 4.18 us -> 0 us
    unnamed x2 -> x0, local copies, waits for them, and re-layouts: 4.18 us -> none
    pallas_call x0 -> x1, Pallas kernels: none -> 3.77 us  [shards(): pl.pallas_call(functools.partial(place_rows, place_dims), grid=(columns /...]
    pallas_call x1, Pallas kernels: 84.2 us -> 81.3 us  [shards(): pl.pallas_call(functools.partial(kernel, dims), out_shape=(jax.ShapeDtype...]
where the time goes in v3:
time: 85.9 us; the launch traced here: 85.7 us
  Pallas kernels  85 us (99%)
    pallas_call x1, Pallas kernels, shards(): pl.pallas_call(functools.partial(kernel, dims), out_shape=(jax.ShapeDtype...  81.3 us
    pallas_call x1, Pallas kernels, shards(): pl.pallas_call(functools.partial(place_rows, place_dims), grid=(columns /...  3.77 us

profile of v3, /device:TPU:0, one launch (start us, length us, event | category | flops | bytes accessed | tf_op | source)
XLA Modules:
  0.0 85.7 jit_solution(11015121627095890690)
XLA Ops:
  0.6 81.3 %shard_map.122 = (bf16[4,96,2048]{2,1,0:T(8,128)(2,1)}, bf16[128,128]{1,0:T(8,128)(2,1)}) custom-call(s32[2,4]{1,0:T(2,128)} %table.1, s32[1,32]{1,0:T(1,128)} %bitcast.19, bf16[8,256,128]{2,1,0:T(8,128)(2,1)} %bitcast.11, bf16[8,256,128]{2,1,0:T(8,128)(2,1)} %bitcast.12, bf16[1024,128]{1,0:T(8,128)(2,1)} %bitcast.13, bf16[512,128]{1,0:T(8,128)(2,1)} %bitcast.14, ...), custom_call_target="tpu_custom_call" | custom-call | flops 2147483648 | bytes 16777216 | tf_op jit(solution)/shard_map/pallas_call | solution.py:674
  81.9 3.8 %shard_map.123 = (bf16[256,2048]{1,0:T(8,128)(2,1)}, bf16[128,2048]{1,0:T(8,128)(2,1)}) custom-call(bf16[128,128]{1,0:T(8,128)(2,1)} %get-tuple-element.6.place, bf16[4,96,2048]{2,1,0:T(8,128)(2,1)} %get-tuple-element.7.summed), custom_call_target="tpu_custom_call" | custom-call | flops 67108864 | bytes 3145728 | tf_op jit(solution)/shard_map/pallas_call | solution.py:745

commit v4 on v3

--- a/solution.py
+++ b/solution.py
@@ -407,9 +407,9 @@
             block_rows[b, start : start + pb, cols] = attended[d, b, sb : sb + pb]
 
     def piece(g, o):
-        b, half = g // 2, g % 2
+        b, part_of = g // 4, g % 4
         row = 0 if by_cols else o * crows
-        col = (2 * o + half if by_cols else half) * ccols
+        col = (4 * o + part_of if by_cols else part_of) * ccols
         return b, slice(row, row + crows), slice(col, col + ccols)
 
     def shift_right(g, o, to):
@@ -553,18 +553,21 @@
         if b >= 1:
             forward_all(b - 1)
         if b >= 2:
-            tick(2 * (b - 2) + 1)
+            tick(4 * (b - 2) + 2)
+            tick(4 * (b - 2) + 3)
         attend_half(b, 1)
         to_sibling(b).start()
         for e in range(1, chips):
             to_far(e, b).start()
         if b >= 1:
             collect(b - 1)
-            tick(2 * (b - 1))
+            tick(4 * (b - 1))
+            tick(4 * (b - 1) + 1)
     forward_all(nb - 1)
-    tick(2 * (nb - 2) + 1)
+    tick(4 * (nb - 2) + 2)
+    tick(4 * (nb - 2) + 3)
     collect(nb - 1)
-    for t in range(2 * (nb - 1), groups + 2 * (heads - 1)):
+    for t in range(4 * (nb - 1), groups + 2 * (heads - 1)):
         tick(t)
 
     for d in range(1, ctx):
@@ -644,11 +647,11 @@
     picked = each * steps
     features, columns = out_weight.shape
     nb = 4
-    groups = 2 * nb
+    groups = 4 * nb
     brows = (prompts * span + steps * samples) // nb
-    by_cols = columns // heads >= 256
+    by_cols = columns // heads >= 512
     crows = brows if by_cols else brows // heads
-    ccols = (columns // heads if by_cols else columns) // 2
+    ccols = (columns // heads if by_cols else columns) // 4
 
     dims = (
         ctx,

time: 85.9 us -> 101 us (1.18)
  Pallas kernels: 85 us -> 99.7 us
    pallas_call x1, Pallas kernels: 81.3 us -> 95.9 us  [shards(): pl.pallas_call(functools.partial(kernel, dims), out_shape=(jax.ShapeDtype...]
where the time goes in v4:
time: 101 us; the launch traced here: 100 us
  Pallas kernels  99.7 us (99%)
    pallas_call x1, Pallas kernels, shards(): pl.pallas_call(functools.partial(kernel, dims), out_shape=(jax.ShapeDtype...  95.9 us
    pallas_call x1, Pallas kernels, shards(): pl.pallas_call(functools.partial(place_rows, place_dims), grid=(columns /...  3.77 us

profile of v4, /device:TPU:0, one launch (start us, length us, event | category | flops | bytes accessed | tf_op | source)
XLA Modules:
  0.0 100.3 jit_solution(13633608997730690359)
XLA Ops:
  0.6 95.9 %shard_map.122 = (bf16[4,96,2048]{2,1,0:T(8,128)(2,1)}, bf16[128,128]{1,0:T(8,128)(2,1)}) custom-call(s32[2,4]{1,0:T(2,128)} %table.1, s32[1,32]{1,0:T(1,128)} %bitcast.19, bf16[8,256,128]{2,1,0:T(8,128)(2,1)} %bitcast.11, bf16[8,256,128]{2,1,0:T(8,128)(2,1)} %bitcast.12, bf16[1024,128]{1,0:T(8,128)(2,1)} %bitcast.13, bf16[512,128]{1,0:T(8,128)(2,1)} %bitcast.14, ...), custom_call_target="tpu_custom_call" | custom-call | flops 2147483648 | bytes 16777216 | tf_op jit(solution)/shard_map/pallas_call | solution.py:677
  96.6 3.8 %shard_map.123 = (bf16[256,2048]{1,0:T(8,128)(2,1)}, bf16[128,2048]{1,0:T(8,128)(2,1)}) custom-call(bf16[128,128]{1,0:T(8,128)(2,1)} %get-tuple-element.6.place, bf16[4,96,2048]{2,1,0:T(8,128)(2,1)} %get-tuple-element.7.summed), custom_call_target="tpu_custom_call" | custom-call | flops 67108864 | bytes 3145728 | tf_op jit(solution)/shard_map/pallas_call | solution.py:748
